TPU v7x, 128 devices: a whole 4x4x4 slice. The times are simulated.
128 devices in a mesh: expert: 32 (over y, x, core), dp: 4 (over z).
Axes of the slice: x: 4, y: 4, z: 4, core: 2. Of those that a mesh axis runs over, the one named last changes fastest.
Arguments:
- tokens: bfloat16 [16384, 7168], P(('expert', 'dp')), may hold values from -6 to 6
- routes: int32 [16384, 8], P(('expert', 'dp')), may hold values from 0 to 31, all different within a row; in each aligned block of 128 rows (0 to 127, 128 to 255, ...) at most 40 rows name the same one
- slab_start: int32 [32], replicated, may hold values from 0 to 6720, as said below
Outputs:
- gram_slab: float32 [32, 448, 7168], P('expert', None, 'dp')
Inputs may be any that keep to these rules, and one draw needn't show every extreme that they name: `routes`: within the rows of one device no expert is named by more than 40 rows, a bound that some block reaches of them; every expert is named somewhere. `slab_start`: multiples of 8.
All inputs are finite; a program needn't handle non-finite values.
Results may differ from a plain program's by a relative error of at most 0.0003.
Values may be sent and summed in bfloat16 or wider, within the bound.
A program may use at most 256 MiB of HBM per device.

v0:
```python
import jax
import jax.numpy as jnp
from jax import lax
from jax.sharding import PartitionSpec as P

SLAB = 448
CAP = 40


def shards(tokens, routes, slab_start):
    owners = lax.axis_size("expert")
    experts = slab_start.shape[0]
    per_owner = experts // owners
    count_tok, width = tokens.shape
    labels = jnp.arange(experts, dtype=jnp.int32)
    assigned = jnp.sum((routes[:, :, None] == labels[None, None, :]).astype(jnp.int32), axis=1)
    position = jnp.cumsum(assigned, axis=0) - 1
    matched = (assigned[:, :, None] == 1) & (
        position[:, :, None] == jnp.arange(CAP, dtype=jnp.int32)[None, None, :]
    )
    filled = jnp.any(matched, axis=0)
    source = jnp.sum(
        matched.astype(jnp.int32) * jnp.arange(count_tok, dtype=jnp.int32)[:, None, None], axis=0
    )
    picked = jnp.take(tokens, source.reshape(-1), axis=0).reshape(experts, CAP, width)
    per_expert = jnp.where(filled[:, :, None], picked, jnp.zeros_like(picked))
    totals = lax.psum(jnp.sum(assigned, axis=0), ("expert", "dp"))
    first_owned = lax.axis_index("expert") * per_owner
    arrived = lax.all_to_all(per_expert, "expert", split_axis=0, concat_axis=0, tiled=True)
    arrived = arrived.reshape(owners, per_owner, CAP, width)
    routed = arrived[:, 0].reshape(owners * CAP, width)
    start = lax.dynamic_index_in_dim(slab_start, first_owned + 0, keepdims=False)
    total = lax.dynamic_index_in_dim(totals, first_owned + 0, keepdims=False).astype(jnp.float32)
    window = lax.dynamic_slice_in_dim(routed, start, SLAB, 1)
    partial_gram = lax.dot_general(
        window, routed, (((0,), (0,)), ((), ())), preferred_element_type=jnp.float32
    )
    share = lax.psum_scatter(partial_gram, "dp", scatter_dimension=1, tiled=True)
    results = [share / total]
    return jnp.stack(results, axis=0)


def solution(mesh):
    placed = (P(("expert", "dp"), None), P(("expert", "dp"), None), P())
    return jax.shard_map(
        shards, mesh=mesh, in_specs=placed, out_specs=P("expert", None, "dp"), check_vma=False
    )
```

profile of v0, /device:TPU:1, one launch (start us, length us, event | category | flops | bytes accessed | tf_op | source)
XLA Modules:
  0.0 422.5 jit_solution(9209829764638853261)
XLA Ops:
  6.5 0.0 copy-start
  6.5 0.9 convert_reduce_fusion
  7.5 0.1 copy.5
  7.6 0.2 reduce_window_sum.11
  7.8 0.1 copy.6
  7.8 0.6 select_reduce_fusion
  8.5 0.1 reshape.57
  8.6 0.6 fusion.3
  9.3 0.0 copy-done
  9.3 14.0 %gather_fusion = bf16[1280,7168]{1,0:T(8,128)(2,1)} fusion(bf16[128,7168]{1,0:T(8,128)(2,1)S(1)} %copy-done, s32[2048]{0:T(1024)S(1)} %pad_clamp_fusion), kind=kCustom, calls=%fused_computation | custom fusion | bytes 36705280 | tf_op jit(solution)/shard_map/jit(_take)/gather | solution.py:25
  23.3 13.4 %select_select_fusion = bf16[32,40,7168]{2,1,0:T(8,128)(2,1)} fusion(bf16[32,40,7168]{2,1,0:T(8,128)(2,1)} %bitcast.7, pred[32,40]{1,0:T(8,128)(4,1)S(1)} %compare_and_fusion, pred[32,40]{1,0:T(8,128)(4,1)S(1)} %fusion.3), kind=kLoop, calls=%fused_computation.1 | loop fusion | flops 18350080 | bytes 36702720 | tf_op jit(solution)/shard_map/jit(_where)/select_n | solution.py:26
  36.8 0.0 copy-start.2
  36.8 8.8 %all-to-all-start = ((bf16[32,40,7168]{2,1,0:T(8,128)(2,1)}), bf16[32,40,7168]{2,1,0:T(8,128)(2,1)}, u32[]{:S(2)}, u32[]{:S(2)}) async-start(bf16[32,40,7168]{2,1,0:T(8,128)(2,1)} %select_select_fusion), calls=%async_computation | async-start | bytes 36700160 | tf_op jit(solution)/shard_map/all_to_all | solution.py:29
  45.5 0.0 reduce-scatter.2.cloned.1.call-start
  45.6 0.0 copy-done.2
  45.6 0.6 dynamic_slice.10
  48.1 218.4 %all-to-all-done = bf16[32,40,7168]{2,1,0:T(8,128)(2,1)} async-done(((bf16[32,40,7168]{2,1,0:T(8,128)(2,1)}), bf16[32,40,7168]{2,1,0:T(8,128)(2,1)}, u32[]{:S(2)}, u32[]{:S(2)}) %all-to-all-start) | async-done | bytes 18350112 | tf_op jit(solution)/shard_map/all_to_all | solution.py:29
  266.6 0.0 copy-start.1
  266.6 16.0 %fusion = f32[448,7168]{1,0:T(8,128)} fusion(bf16[1280,7168]{1,0:T(8,128)(2,1)} %bitcast.1, s32[]{:T(128)S(6)} %select_n.39), kind=kOutput, calls=%fused_computation.3 | convolution fusion | flops 8220835840 | bytes 32505860 | tf_op jit(solution)/shard_map/dot_general | solution.py:35
  282.6 0.0 reduce-scatter.2.cloned.1.call-update
  282.6 79.7 %psum.7 = s32[32]{0:T(128)S(1)} all-reduce(s32[32]{0:T(128)S(1)} %get-tuple-element.5), channel_id=1, replica_groups=mesh['expert'=32,'dp'=4] {'expert','dp'}, use_global_device_ids=true, to_apply=%region_6.7 | all-reduce | flops 32 | bytes 256 | tf_op jit(solution)/shard_map/psum | solution.py:27
  362.4 0.6 dynamic_slice.12
  363.6 48.2 %reduce-scatter.2.cloned.1.call-done = f32[448,1792]{1,0:T(8,128)} async-done(((f32[448,7168]{1,0:T(8,128)}), f32[448,1792]{1,0:T(8,128)}) %reduce-scatter.2.cloned.1.call-update) | async-done | bytes 3211280 | tf_op jit(solution)/shard_map/reduce_scatter | solution.py:38
  411.8 3.8 divide_bitcast_fusion
  415.6 0.0 copy-done.1
  (5 shorter events, 0.1 us)
Async XLA Ops:
  6.5 2.7 copy-start
  36.8 8.8 %copy-start.2 = (s32[32]{0:T(128)S(1)}, s32[32]{0:T(128)}, u32[]{:S(2)}) copy-start(s32[32]{0:T(128)} %param.5) | copy-start | bytes 388
  36.8 229.8 %all-to-all-start = ((bf16[32,40,7168]{2,1,0:T(8,128)(2,1)}), bf16[32,40,7168]{2,1,0:T(8,128)(2,1)}, u32[]{:S(2)}, u32[]{:S(2)}) async-start(bf16[32,40,7168]{2,1,0:T(8,128)(2,1)} %select_select_fusion), calls=%async_computation | async-start | bytes 36700160 | tf_op jit(solution)/shard_map/all_to_all | solution.py:29
  45.5 366.3 %reduce-scatter.2.cloned.1.call-start = ((), (), s32[]{:S(2)}) async-start(), calls=%async_computation.2 | async-start | bytes 16056320 | tf_op jit(solution)/shard_map/reduce_scatter | solution.py:38
  266.6 149.0 %copy-start.1 = (bf16[128,7168]{1,0:T(8,128)(2,1)S(1)}, bf16[128,7168]{1,0:T(8,128)(2,1)}, u32[]{:S(2)}) copy-start(bf16[128,7168]{1,0:T(8,128)(2,1)} %param.3) | copy-start | bytes 5505028
Sparse Core Ops, SparseCore 0:
  282.8 128.9 reduce-scatter.1
where the time goes:
time: 423 us; the launch traced here: 422 us
  waiting for transfers between devices  267 us (63%)
  blocking collectives  79.7 us (19%)
  other arithmetic  19.7 us (5%)
  between operations  16.1 us (4%)
  matrix products  16 us (4%)
  local copies, waits for them, and re-layouts  15.5 us (4%)
  starting transfers between devices  8.81 us (2%)
    all_to_all x1, waiting for transfers between devices, shards(): lax.all_to_all(per_expert, 'expert', split_axis=0, concat_axis=0, tiled=T...  218 us
    psum x1, blocking collectives, shards(): totals = lax.psum(jnp.sum(assigned, axis=0), ('expert', 'dp'))  79.7 us
    reduce_scatter x1, waiting for transfers between devices, shards(): lax.psum_scatter(partial_gram, 'dp', scatter_dimension=1, tiled=True)  48.2 us
    dot_general x1, matrix products, shards(): lax.dot_general(window, routed, (((0,), (0,)), ((), ())), preferred_eleme...  16 us
    gather x1, local copies, waits for them, and re-layouts, shards(): jnp.take(tokens, source.reshape(-1), axis=0).reshape(experts, CAP, width)  14 us
    select_n x1, other arithmetic, shards(): per_expert = jnp.where(filled[:, :, None], picked, jnp.zeros_like(picked))  13.4 us
    all_to_all x1, starting transfers between devices, shards(): lax.all_to_all(per_expert, 'expert', split_axis=0, concat_axis=0, tiled=T...  8.77 us
  transfers between devices with their start and end apart: 2, of which 2 were waited for; matrix products, arithmetic and copies ran while one was open for 0% of the time, Pallas kernels for 0%

commit v1 on v0

v1 whole, which is shorter than its diff:
```python
import functools

import jax
import jax.numpy as jnp
from jax import lax
from jax.experimental import pallas as pl
from jax.experimental.pallas import tpu as pltpu
from jax.sharding import PartitionSpec as P

MESH = pl.DeviceIdType.MESH
SLAB = 448
CAP = 40
PAIR = 2 * CAP
WIDE = 512
RING = 4
TOK = 128
WIDTH = 7168
BLOCK = WIDTH // RING
CHUNK = 256
CHUNKS = BLOCK // CHUNK
ROWS = RING * RING * 2 * TOK
GROUPS = 4
OFFSETS = (2, 1, 3, 0)
SCALE_ROWS = 112
HALF = SLAB // 2
SPAN = 640

ORDER = ("P", "XB", "XA", "Z", "WZ", "WZF", "C", "EXP", "U")
SCHEDULE = (
    "XA0", "P0", "XA1", "P1", "P2", "WZ0", "XB0", "XA2", "Z3", "P3", "WZ1", "WZF0", "C0", "XB1", "XA3", "Z4", "WZ2",
    "EXP0", "U00", "WZF1", "C1", "XB2", "XA4", "Z5", "WZ3", "EXP1", "U01", "U10", "U11", "WZF2", "C2", "XB3", "XA5",
    "Z6", "EXP2", "U02", "U12", "U20", "U21", "U22", "WZF3", "C3", "XB4", "XA6", "U03", "U13", "U23", "EXP3", "U30",
    "C4", "XB5", "U04", "U14", "U24", "U31", "C5", "XB6", "U05", "U15", "U25", "U32", "C6", "U06", "U16", "U26",
    "U33", "U34", "U35", "U36",
)


def plan():
    tables = {name: {} for name in ORDER}
    step, last = 0, -1
    for item in SCHEDULE:
        name = item.rstrip("0123456789")
        digits = item[len(name):]
        value = int(digits[0]) * CHUNKS + int(digits[1]) if name == "U" else int(digits)
        rank = ORDER.index(name)
        if rank <= last:
            step += 1
        last = rank
        tables[name][step] = value
    return tables, step + 1


def looked_up(table, step):
    value = jnp.int32(-1)
    for at, entry in table.items():
        value = jnp.where(step == at, jnp.int32(entry), value)
    return value


def offset_of(group):
    value = jnp.int32(OFFSETS[0])
    for index in range(1, GROUPS):
        value = jnp.where(group == index, jnp.int32(OFFSETS[index]), value)
    return value


def gram_kernel(
    start_ref, routes_ref, tok_ref, out_ref,
    both, listed, slots, packed, win, wide, cols, part, quant, scale, half_q, half_s, full_q, full_s, hits,
    pair_s, pair_r, own_s, z_s, z_r, zl_s, xa_s, xa_r, xb_s, xb_r, c_s, c_r,
    wx_s, wx_r, wz_s, wz_r, wf_s, wf_r, hq_s, hq_r, hs_s, hs_r, fq_s, fq_r, fs_s, fs_r,
):
    expert = lax.axis_index("expert")
    z = lax.axis_index("dp")
    core = expert % 2
    x = (expert // 2) % RING
    y = expert // (2 * RING)

    def device(dy=0, dx=0, dz=0, dc=0):
        ey, ex, ec = (y + dy) % RING, (x + dx) % RING, (core + dc) % 2
        return ((ey * RING + ex) * 2 + ec, (z + dz) % RING)

    def remote(src, dst, send, recv, to):
        return pltpu.make_async_remote_copy(
            src_ref=src, dst_ref=dst, send_sem=send, recv_sem=recv, device_id=to, device_id_type=MESH
        )

    def pair_copies():
        return (
            remote(routes_ref, listed.at[core], pair_s.at[0], pair_r.at[0], device(dc=1)),
            remote(tok_ref, both.at[pl.ds(core * TOK, TOK)], pair_s.at[1], pair_r.at[1], device(dc=1)),
        )

    def own_copy():
        return pltpu.make_async_copy(tok_ref, both.at[pl.ds(core * TOK, TOK)], own_s)

    def z_copy(k, d):
        first = pl.multiple_of(((z + d) % RING) * BLOCK + k * CHUNK, 128)
        return remote(
            tok_ref.at[:, pl.ds(first, CHUNK)], cols.at[k, core, x, z], z_s.at[k, d - 1], z_r.at[k, d - 1], device(dz=d)
        )

    def z_local(k):
        first = pl.multiple_of(z * BLOCK + k * CHUNK, 128)
        return pltpu.make_async_copy(tok_ref.at[:, pl.ds(first, CHUNK)], cols.at[k, core, x, z], zl_s.at[k])

    def xa_copy(k, way):
        here = cols.at[k, core, x]
        return remote(here, here, xa_s.at[k, way], xa_r.at[k, way], device(dx=1 if way == 0 else 3))

    def xb_copy(k, way):
        origin = (x + (3 if way == 0 else 1)) % RING
        here = cols.at[k, core, origin, pl.ds(2 * way, 2)]
        return remote(here, here, xb_s.at[k, way], xb_r.at[k, way], device(dx=1 if way == 0 else 3))

    def c_copy(k):
        here = cols.at[k, core]
        return remote(here, here, c_s.at[k], c_r.at[k], device(dc=1))

    def wx_copy(g, d):
        return remote(
            packed.at[g * RING + d], win.at[g, z, x], wx_s.at[g, d - 1], wx_r.at[g, d - 1], device(dx=d)
        )

    def wz_copy(g, way):
        here = win.at[g, z]
        return remote(here, here, wz_s.at[g, way], wz_r.at[g, way], device(dz=1 if way == 0 else 3))

    def wf_copy(g, way):
        origin = (z + (3 if way == 0 else 1)) % RING
        here = win.at[g, origin, pl.ds(2 * way, 2)]
        return remote(here, here, wf_s.at[g, way], wf_r.at[g, way], device(dz=1 if way == 0 else 3))

    def half_copies(k, way):
        to = device(dy=1 if way == 0 else 3)
        return (
            remote(quant.at[0, k, pl.ds(way * HALF, HALF)], half_q.at[way, k], hq_s.at[way, k], hq_r.at[way, k], to),
            remote(scale.at[0, k], half_s.at[way, k], hs_s.at[way, k], hs_r.at[way, k], to),
        )

    def full_copies(g, k):
        way = g - 1
        to = device(dy=jnp.where(g == 1, 1, 3))
        return (
            remote(quant.at[g, k], full_q.at[way, k], fq_s.at[way, k], fq_r.at[way, k], to),
            remote(scale.at[g, k], full_s.at[way, k], fs_s.at[way, k], fs_r.at[way, k], to),
        )

    barrier = pltpu.get_barrier_semaphore()
    peers = [device(dc=1), device(dy=1), device(dy=3)]
    peers += [device(dx=d) for d in (1, 2, 3)] + [device(dz=d) for d in (1, 2, 3)]
    for peer in peers:
        pl.semaphore_signal(barrier, inc=1, device_id=peer, device_id_type=MESH)
    pl.semaphore_wait(barrier, len(peers))

    def send_z(k):
        for d in (1, 3, 2):
            z_copy(k, d).start()
        z_local(k).start()

    for copy in pair_copies():
        copy.start()
    own_copy().start()
    for k in range(3):
        send_z(jnp.int32(k))
    listed[core] = routes_ref[...]

    def take_xa(k):
        for d in (1, 2, 3):
            z_copy(k, d).wait_recv()
        z_local(k).wait()
        for way in (0, 1):
            xa_copy(k, way).start()

    def take_xb(k):
        for way in (0, 1):
            xa_copy(k, way).wait_recv()
            xb_copy(k, way).start()

    def take_c(k):
        for way in (0, 1):
            xb_copy(k, way).wait_recv()
        c_copy(k).start()

    def find_slots():
        for copy in pair_copies():
            copy.wait_recv()
        own_copy().wait()
        named = jnp.concatenate([listed[0], listed[1]], axis=1)
        row = lax.broadcasted_iota(jnp.int32, (GROUPS * RING, 2 * TOK), 0)
        group, step = row // RING, row % RING
        away = jnp.where(group == 0, OFFSETS[0], jnp.where(group == 1, OFFSETS[1], jnp.where(group == 2, OFFSETS[2], OFFSETS[3])))
        label = (((y + away) % RING) * RING + (x + step) % RING) * 2 + core
        hit = jnp.zeros((GROUPS * RING, 2 * TOK), jnp.float32)
        for choice in range(named.shape[0]):
            hit += jnp.where(named[choice:choice + 1, :] == label, 1.0, 0.0)
        before = lax.broadcasted_iota(jnp.int32, (2 * TOK, 2 * TOK), 0) < lax.broadcasted_iota(
            jnp.int32, (2 * TOK, 2 * TOK), 1
        )
        rank = jnp.dot(
            hit.astype(jnp.bfloat16), jnp.where(before, 1.0, 0.0).astype(jnp.bfloat16), preferred_element_type=jnp.float32
        )
        slots[...] = jnp.where(hit > 0.0, rank, -1.0)

    def take_p(g):
        pl.when(g == 0)(find_slots)
        slot = lax.broadcasted_iota(jnp.int32, (PAIR, 2 * TOK), 0).astype(jnp.float32)
        number = (lax.broadcasted_iota(jnp.int32, (2 * TOK, 128), 0) + 1).astype(jnp.float32).astype(jnp.bfloat16)
        lane = lax.broadcasted_iota(jnp.int32, (PAIR, 128), 1)
        source = lax.broadcasted_iota(jnp.int32, (SPAN, WIDE), 0)
        target = lax.broadcasted_iota(jnp.int32, (SPAN, WIDE), 1)
        for d in (2, 1, 3, 0):
            row = g * RING + d
            chosen = jnp.where(slots[pl.ds(row, 1), :] == slot, 1.0, 0.0).astype(jnp.bfloat16)
            label = (((y + offset_of(g)) % RING) * RING + (x + d) % RING) * 2 + core
            start = start_ref[label]
            tile = jnp.minimum(lax.div(start, jnp.int32(128)), (WIDTH - SPAN) // 128)
            shift = start - tile * 128
            first = tile * 128
            rows = both[:, pl.ds(first, SPAN)]
            picked = jnp.dot(chosen, rows, preferred_element_type=jnp.float32)
            moved = jnp.where(source == target + shift, 1.0, 0.0).astype(jnp.bfloat16)
            picked = jnp.dot(picked.astype(jnp.bfloat16), moved, preferred_element_type=jnp.float32)
            index = jnp.dot(chosen, number, preferred_element_type=jnp.float32)
            last = jnp.where(lane >= SLAB - 384, index, picked[:, 384:512])
            value = jnp.concatenate([picked[:, :384], last], axis=1).astype(jnp.bfloat16)
            if d == 0:
                win[g, z, x] = value
            else:
                packed[row] = value
                wx_copy(g, d).start()

    def take_wz(g):
        for d in (1, 2, 3):
            wx_copy(g, d).wait_recv()
        for way in (0, 1):
            wz_copy(g, way).start()

    def take_wzf(g):
        for way in (0, 1):
            wz_copy(g, way).wait_recv()
            wf_copy(g, way).start()

    def take_exp(g):
        for way in (0, 1):
            wf_copy(g, way).wait_recv()
        token = (lax.broadcasted_iota(jnp.int32, (PAIR, 2 * TOK), 1) + 1).astype(jnp.float32)

        def one(place, total):
            held = win[g, place % RING, place // RING]
            index = held[:, SLAB:SLAB + 1].astype(jnp.float32)
            chosen = jnp.where(index == token, 1.0, 0.0)
            full = lax.dot_general(
                held[:, :SLAB], chosen.astype(jnp.bfloat16), (((0,), (0,)), ((), ())), preferred_element_type=jnp.float32
            ).astype(jnp.bfloat16)
            for side in (0, 1):
                at = pl.multiple_of((side * RING * RING + place) * TOK, 128)
                wide[g, :, pl.ds(at, TOK)] = full[:, side * TOK:(side + 1) * TOK]
            return total + jnp.sum(chosen, axis=0, keepdims=True)

        hits[g] = lax.fori_loop(0, RING * RING, one, jnp.zeros((1, 2 * TOK), jnp.float32))

    def restored(block_q, row_scale):
        return block_q.astype(jnp.int32).astype(jnp.float32) * row_scale

    def take_u(unit):
        g, k = unit // CHUNKS, unit % CHUNKS

        @pl.when(g == 0)
        def _():
            c_copy(k).wait_recv()

        tokens = cols[k].reshape(ROWS, CHUNK)
        part[...] = jnp.dot(wide[g], tokens, preferred_element_type=jnp.float32)

        @pl.when(g == 3)
        def _():
            out_ref[:, pl.ds(pl.multiple_of(k * CHUNK, 128), CHUNK)] = part[...]

        @pl.when(g < 3)
        def _():
            scale[g, k, pl.ds(7, 1), :] = hits[g]

        for way in (0, 1):
            @pl.when(g == 1 + way)
            def _():
                for copy in half_copies(k, way):
                    copy.wait_recv()
                for piece in range(2):
                    rows = pl.ds(way * HALF + piece * SCALE_ROWS, SCALE_ROWS)
                    part[rows, :] += restored(
                        half_q[way, k, pl.ds(piece * SCALE_ROWS, SCALE_ROWS), :],
                        half_s[way, k, pl.ds(2 * way + piece, 1), :],
                    )
                if way == 0:
                    scale[g, k, pl.ds(7, 1), :] = hits[g] + half_s[way, k, pl.ds(7, 1), :]

        @pl.when(g < 3)
        def _():
            for piece in range(SLAB // SCALE_ROWS):
                rows = pl.ds(piece * SCALE_ROWS, SCALE_ROWS)
                block = part[rows, :]
                most = jnp.max(jnp.abs(block), axis=0, keepdims=True)
                factor = jnp.where(most > 0.0, 32767.0 / jnp.where(most > 0.0, most, 1.0), 0.0)
                quant[g, k, rows, :] = jnp.round(block * factor).astype(jnp.int32).astype(jnp.int16)
                scale[g, k, pl.ds(piece, 1), :] = most * (1.0 / 32767.0)

        @pl.when(g == 0)
        def _():
            for way in (0, 1):
                for copy in half_copies(k, way):
                    copy.start()

        @pl.when((g == 1) | (g == 2))
        def _():
            for copy in full_copies(g, k):
                copy.start()

    actions = {
        "P": take_p, "XB": take_xb, "XA": take_xa, "Z": send_z, "WZ": take_wz, "WZF": take_wzf, "C": take_c,
        "EXP": take_exp, "U": take_u,
    }
    tables, steps = plan()

    def one_step(step, carry):
        for name in ORDER:
            value = looked_up(tables[name], step)
            pl.when(value >= 0)(functools.partial(actions[name], value))
        return carry

    lax.fori_loop(0, steps, one_step, 0)

    def finish(k, carry):
        for g in (1, 2):
            for copy in full_copies(jnp.int32(g), k):
                copy.wait_recv()
        count = hits[3] + full_s[0, k, pl.ds(7, 1), :] + full_s[1, k, pl.ds(7, 1), :]
        inverse = 1.0 / jnp.sum(count, axis=1, keepdims=True)
        at = pl.ds(pl.multiple_of(k * CHUNK, 128), CHUNK)
        for piece in range(SLAB // SCALE_ROWS):
            rows = pl.ds(piece * SCALE_ROWS, SCALE_ROWS)
            total = out_ref[rows, at]
            for way in (0, 1):
                total += restored(full_q[way, k, rows, :], full_s[way, k, pl.ds(piece, 1), :])
            out_ref[rows, at] = total * inverse
        return carry

    lax.fori_loop(0, CHUNKS, finish, 0)

    for copy in pair_copies():
        copy.wait_send()

    def drain(k, carry):
        for d in (1, 2, 3):
            z_copy(k, d).wait_send()
        for way in (0, 1):
            xa_copy(k, way).wait_send()
            xb_copy(k, way).wait_send()
            for copy in half_copies(k, way):
                copy.wait_send()
        c_copy(k).wait_send()
        for g in (1, 2):
            for copy in full_copies(jnp.int32(g), k):
                copy.wait_send()
        return carry

    lax.fori_loop(0, CHUNKS, drain, 0)

    def drain_windows(g, carry):
        for d in (1, 2, 3):
            wx_copy(g, d).wait_send()
        for way in (0, 1):
            wz_copy(g, way).wait_send()
            wf_copy(g, way).wait_send()
        return carry

    lax.fori_loop(0, GROUPS, drain_windows, 0)


def shards(tokens, routes, slab_start):
    dma = pltpu.SemaphoreType.DMA
    bf16, f32, i16 = jnp.bfloat16, jnp.float32, jnp.int16
    pairs = [(CHUNKS, 2)] * 2
    result = pl.pallas_call(
        gram_kernel,
        out_shape=jax.ShapeDtypeStruct((SLAB, BLOCK), f32),
        in_specs=[
            pl.BlockSpec(memory_space=pltpu.SMEM),
            pl.BlockSpec(memory_space=pltpu.VMEM),
            pl.BlockSpec(memory_space=pl.ANY),
        ],
        out_specs=pl.BlockSpec(memory_space=pltpu.VMEM),
        scratch_shapes=[
            pltpu.VMEM((2 * TOK, WIDTH), bf16),
            pltpu.VMEM((2, 8, TOK), jnp.int32),
            pltpu.VMEM((GROUPS * RING, 2 * TOK), f32),
            pltpu.VMEM((GROUPS * RING, PAIR, WIDE), bf16),
            pltpu.VMEM((GROUPS, RING, RING, PAIR, WIDE), bf16),
            pltpu.VMEM((GROUPS, SLAB, ROWS), bf16),
            pltpu.VMEM((CHUNKS, 2, RING, RING, TOK, CHUNK), bf16),
            pltpu.VMEM((SLAB, CHUNK), f32),
            pltpu.VMEM((3, CHUNKS, SLAB, CHUNK), i16),
            pltpu.VMEM((3, CHUNKS, 8, CHUNK), f32),
            pltpu.VMEM((2, CHUNKS, HALF, CHUNK), i16),
            pltpu.VMEM((2, CHUNKS, 8, CHUNK), f32),
            pltpu.VMEM((2, CHUNKS, SLAB, CHUNK), i16),
            pltpu.VMEM((2, CHUNKS, 8, CHUNK), f32),
            pltpu.VMEM((GROUPS, 1, 2 * TOK), f32),
            dma((2,)), dma((2,)), dma(()),
            dma((CHUNKS, 3)), dma((CHUNKS, 3)), dma((CHUNKS,)),
            dma((CHUNKS, 2)), dma((CHUNKS, 2)), dma((CHUNKS, 2)), dma((CHUNKS, 2)), dma((CHUNKS,)), dma((CHUNKS,)),
            dma((GROUPS, 3)), dma((GROUPS, 3)), dma((GROUPS, 2)), dma((GROUPS, 2)), dma((GROUPS, 2)), dma((GROUPS, 2)),
            dma((2, CHUNKS)), dma((2, CHUNKS)), dma((2, CHUNKS)), dma((2, CHUNKS)),
            dma((2, CHUNKS)), dma((2, CHUNKS)), dma((2, CHUNKS)), dma((2, CHUNKS)),
        ],
        compiler_params=pltpu.CompilerParams(
            collective_id=0, has_side_effects=True, vmem_limit_bytes=62 * 2**20
        ),
        name="gram",
    )(slab_start, routes.T, tokens)
    return result[None]


def solution(mesh):
    placed = (P(("expert", "dp"), None), P(("expert", "dp"), None), P())
    return jax.shard_map(
        shards, mesh=mesh, in_specs=placed, out_specs=P("expert", None, "dp"), check_vma=False
    )
```

time: 423 us -> 162 us (0.38)
  waiting for transfers between devices: 267 us -> 0 us
  Pallas kernels: 0 us -> 158 us
  blocking collectives: 79.7 us -> 0 us
  other arithmetic: 19.7 us -> 0 us
  between operations: 16.1 us -> 0.01 us
  matrix products: 16 us -> 0 us
  local copies, waits for them, and re-layouts: 15.5 us -> 3.8 us
  starting transfers between devices: 8.81 us -> 0 us
    all_to_all x1 -> x0, waiting for transfers between devices: 218 us -> none  [shards(): lax.all_to_all(per_expert, 'expert', split_axis=0, concat_axis=0, tiled=T...]
    pallas_call x0 -> x1, Pallas kernels: none -> 158 us  [shards(): pl.pallas_call(gram_kernel, out_shape=jax.ShapeDtypeStruct((SLAB, BLOCK),...]
    psum x1 -> x0, blocking collectives: 79.7 us -> none  [shards(): totals = lax.psum(jnp.sum(assigned, axis=0), ('expert', 'dp'))]
    reduce_scatter x1 -> x0, waiting for transfers between devices: 48.2 us -> none  [shards(): lax.psum_scatter(partial_gram, 'dp', scatter_dimension=1, tiled=True)]
    dot_general x1 -> x0, matrix products: 16 us -> none  [shards(): lax.dot_general(window, routed, (((0,), (0,)), ((), ())), preferred_eleme...]
    gather x1 -> x0, local copies, waits for them, and re-layouts: 14 us -> none  [shards(): jnp.take(tokens, source.reshape(-1), axis=0).reshape(experts, CAP, width)]
    select_n x2 -> x0, other arithmetic: 13.5 us -> none  [the longest x1 13.4 us: shards(): per_expert = jnp.where(filled[:, :, None], picked, jnp.zeros_like(picked))]
    all_to_all x1 -> x0, starting transfers between devices: 8.77 us -> none  [shards(): lax.all_to_all(per_expert, 'expert', split_axis=0, concat_axis=0, tiled=T...]
  transfers between devices with their start and end apart: 2 -> 0, of which waited for: 2 -> 0; matrix products, arithmetic and copies ran while one was open for 0% -> 0% of each run, Pallas kernels for 0% -> 0%
where the time goes in v1:
time: 162 us
  Pallas kernels  158 us (98%)
  local copies, waits for them, and re-layouts  3.8 us (2%)
    pallas_call x1, Pallas kernels, shards(): pl.pallas_call(gram_kernel, out_shape=jax.ShapeDtypeStruct((SLAB, BLOCK),...  158 us
    unnamed x1, local copies, waits for them, and re-layouts  3.8 us

profile of v1, /device:TPU:1, one launch (start us, length us, event | category | flops | bytes accessed | tf_op | source)
XLA Modules:
  0.0 161.7 jit_solution(1834437774323870027)
XLA Ops:
  0.0 157.9 %gram.1 = f32[448,1792]{1,0:T(8,128)} custom-call(s32[32]{0:T(128)} %start_ref.1, s32[8,128]{1,0:T(8,128)} %bitcast.3, bf16[128,7168]{1,0:T(8,128)(2,1)} %tok_ref.1), custom_call_target="tpu_custom_call" | custom-call | tf_op jit(solution)/shard_map/gram/pallas_call | solution.py:384
  157.9 3.8 %copy.5 = f32[1,448,1792]{2,1,0:T(8,128)} copy(f32[1,448,1792]{2,1,0:T(8,128)} %bitcast.2) | data formatting | bytes 6422528

commit v2 on v1

--- a/solution.py
+++ b/solution.py
@@ -25,13 +25,13 @@
 HALF = SLAB // 2
 SPAN = 640
 
-ORDER = ("P", "XB", "XA", "Z", "WZ", "WZF", "C", "EXP", "U")
+ORDER = ("S", "P", "XB", "XA", "Z", "WZ", "WZF", "C", "EXP", "U")
 SCHEDULE = (
-    "XA0", "P0", "XA1", "P1", "P2", "WZ0", "XB0", "XA2", "Z3", "P3", "WZ1", "WZF0", "C0", "XB1", "XA3", "Z4", "WZ2",
-    "EXP0", "U00", "WZF1", "C1", "XB2", "XA4", "Z5", "WZ3", "EXP1", "U01", "U10", "U11", "WZF2", "C2", "XB3", "XA5",
-    "Z6", "EXP2", "U02", "U12", "U20", "U21", "U22", "WZF3", "C3", "XB4", "XA6", "U03", "U13", "U23", "EXP3", "U30",
-    "C4", "XB5", "U04", "U14", "U24", "U31", "C5", "XB6", "U05", "U15", "U25", "U32", "C6", "U06", "U16", "U26",
-    "U33", "U34", "U35", "U36",
+    "XA0", "Z4", "S0", "P2", "Z6", "P0", "P1", "WZ2", "XA1", "XA4", "WZ0", "XB0", "WZF2", "XB1", "WZF0", "WZ1",
+    "XB4", "XA6", "P3", "C0", "EXP2", "C1", "Z3", "EXP0", "C4", "U01", "WZF1", "U00", "U04", "Z5", "XB6", "XA3",
+    "U21", "EXP1", "U10", "U24", "C6", "XA5", "U11", "U06", "WZ3", "XB3", "U20", "XB5", "XA2", "U14", "C3", "U26",
+    "WZF3", "U03", "C5", "U16", "XB2", "U05", "U13", "U23", "C2", "EXP3", "U30", "U02", "U15", "U33", "U25", "U22",
+    "U35", "U12", "U36", "U34", "U31", "U32",
 )
 
 
@@ -182,7 +182,7 @@
             xb_copy(k, way).wait_recv()
         c_copy(k).start()
 
-    def find_slots():
+    def find_slots(_):
         for copy in pair_copies():
             copy.wait_recv()
         own_copy().wait()
@@ -203,7 +203,6 @@
         slots[...] = jnp.where(hit > 0.0, rank, -1.0)
 
     def take_p(g):
-        pl.when(g == 0)(find_slots)
         slot = lax.broadcasted_iota(jnp.int32, (PAIR, 2 * TOK), 0).astype(jnp.float32)
         number = (lax.broadcasted_iota(jnp.int32, (2 * TOK, 128), 0) + 1).astype(jnp.float32).astype(jnp.bfloat16)
         lane = lax.broadcasted_iota(jnp.int32, (PAIR, 128), 1)
@@ -258,7 +257,7 @@
                 wide[g, :, pl.ds(at, TOK)] = full[:, side * TOK:(side + 1) * TOK]
             return total + jnp.sum(chosen, axis=0, keepdims=True)
 
-        hits[g] = lax.fori_loop(0, RING * RING, one, jnp.zeros((1, 2 * TOK), jnp.float32))
+        hits[g] = lax.fori_loop(0, RING * RING, one, jnp.zeros((1, 2 * TOK), jnp.float32), unroll=4)
 
     def restored(block_q, row_scale):
         return block_q.astype(jnp.int32).astype(jnp.float32) * row_scale
@@ -317,7 +316,7 @@
                 copy.start()
 
     actions = {
-        "P": take_p, "XB": take_xb, "XA": take_xa, "Z": send_z, "WZ": take_wz, "WZF": take_wzf, "C": take_c,
+        "S": find_slots, "P": take_p, "XB": take_xb, "XA": take_xa, "Z": send_z, "WZ": take_wz, "WZF": take_wzf, "C": take_c,
         "EXP": take_exp, "U": take_u,
     }
     tables, steps = plan()
@@ -383,7 +382,7 @@
     pairs = [(CHUNKS, 2)] * 2
     result = pl.pallas_call(
         gram_kernel,
-        out_shape=jax.ShapeDtypeStruct((SLAB, BLOCK), f32),
+        out_shape=pltpu.VMEM((SLAB, BLOCK), f32),
         in_specs=[
             pl.BlockSpec(memory_space=pltpu.SMEM),
             pl.BlockSpec(memory_space=pltpu.VMEM),
@@ -414,7 +413,7 @@
             dma((2, CHUNKS)), dma((2, CHUNKS)), dma((2, CHUNKS)), dma((2, CHUNKS)),
         ],
         compiler_params=pltpu.CompilerParams(
-            collective_id=0, has_side_effects=True, vmem_limit_bytes=62 * 2**20
+            collective_id=0, has_side_effects=True, vmem_limit_bytes=56 * 2**20
         ),
         name="gram",
     )(slab_start, routes.T, tokens)

time: 162 us -> 118 us (0.73)
  Pallas kernels: 158 us -> 115 us
  local copies, waits for them, and re-layouts: 3.8 us -> 1.69 us
    pallas_call x1, Pallas kernels: 158 us -> 115 us  [shards(): pl.pallas_call(gram_kernel, out_shape=pltpu.VMEM((SLAB, BLOCK), f32), in_...]
    unnamed x1, local copies, waits for them, and re-layouts: 3.8 us -> 1.69 us
where the time goes in v2:
time: 118 us; the launch traced here: 117 us
  Pallas kernels  115 us (97%)
  local copies, waits for them, and re-layouts  1.69 us (1%)
    pallas_call x1, Pallas kernels, shards(): pl.pallas_call(gram_kernel, out_shape=pltpu.VMEM((SLAB, BLOCK), f32), in_...  115 us

profile of v2, /device:TPU:1, one launch (start us, length us, event | category | flops | bytes accessed | tf_op | source)
XLA Modules:
  0.0 116.8 jit_solution(1912106585891784027)
XLA Ops:
  0.0 115.1 %gram.1 = f32[448,1792]{1,0:T(8,128)S(1)} custom-call(s32[32]{0:T(128)} %start_ref.1, s32[8,128]{1,0:T(8,128)} %bitcast.3, bf16[128,7168]{1,0:T(8,128)(2,1)} %tok_ref.1), custom_call_target="tpu_custom_call" | custom-call | tf_op jit(solution)/shard_map/gram/pallas_call | solution.py:383
  115.1 1.7 %copy.5 = f32[1,448,1792]{2,1,0:T(8,128)} copy(f32[1,448,1792]{2,1,0:T(8,128)S(1)} %bitcast.2) | data formatting | bytes 6422528

commit v3 on v2

v3 whole, which is shorter than its diff:
```python
import jax
import jax.numpy as jnp
from jax import lax
from jax.experimental import pallas as pl
from jax.experimental.pallas import tpu as pltpu
from jax.sharding import PartitionSpec as P

MESH = pl.DeviceIdType.MESH
SLAB = 448
CAP = 40
PAIR = 2 * CAP
FULL = 3 * PAIR
TAIL = 48
RING = 4
TOK = 128
WIDTH = 7168
BLOCK = WIDTH // RING
CHUNK = 256
CHUNKS = BLOCK // CHUNK
PLACES = RING * RING
GROUPS = 4
OFFSETS = (2, 1, 3, 0)
SCALE_ROWS = 112
HALF = SLAB // 2
SPAN = 640

CODES = {
    "U": 0, "V": 28, "XO": 42, "XA": 49, "XB": 56, "C": 63, "Z": 70, "P": 77, "WZ": 81, "WZF": 85, "EXP": 89, "S": 93,
}
SCHEDULE = (
    "XO1", "XO5", "Z5", "XO4", "XO0", "S0", "P0", "P2", "WZ0", "P1", "WZ2", "XA1", "WZF0", "XA5", "XA0", "WZ1",
    "WZF2", "XB5", "XB1", "XB0", "P3", "C5", "EXP0", "XO2", "C1", "XA2", "U05", "WZF1", "XO6", "C0", "U01", "Z4",
    "EXP2", "U25", "U00", "Z6", "EXP1", "U15", "U10", "XB2", "V05", "V15", "U20", "XA4", "U21", "C2", "XA6", "WZ3",
    "V11", "U11", "U02", "V10", "V01", "XB4", "Z3", "XB6", "XO3", "V00", "U12", "U22", "C4", "V02", "XA3", "WZF3",
    "C6", "V12", "U06", "U04", "U26", "XB3", "U16", "U24", "U14", "V16", "C3", "EXP3", "U32", "U03", "U23", "U34",
    "V04", "U13", "U30", "V06", "V03", "V13", "U36", "U31", "V14", "U35", "U33",
)


def plan():
    codes = []
    for item in SCHEDULE:
        name = item.rstrip("0123456789")
        digits = item[len(name):]
        value = int(digits[0]) * CHUNKS + int(digits[1]) if len(digits) == 2 else int(digits)
        codes.append(CODES[name] + value)
    padded = codes + [0] * (-len(codes) % 4)
    words = [sum(padded[at + i] * 128 ** i for i in range(4)) for at in range(0, len(padded), 4)]
    return words, len(codes)


def looked_up(words, step):
    word = jnp.int32(words[0])
    for at in range(1, len(words)):
        word = jnp.where(step // 4 == at, jnp.int32(words[at]), word)
    return lax.shift_right_logical(word, 7 * (step % 4)) % 128


def offset_of(group):
    value = jnp.int32(OFFSETS[0])
    for index in range(1, GROUPS):
        value = jnp.where(group == index, jnp.int32(OFFSETS[index]), value)
    return value


def gram_kernel(
    start_ref, routes_ref, tok_ref, out_ref,
    both, listed, slots, packed, win, chosen, wide, cols, near, part, kept, quant, scale, got_q, got_s, hits,
    pair_s, pair_r, own_s, z_s, z_r, zl_s, xo_s, xo_r, xa_s, xa_r, xb_s, xb_r, ca_s, ca_r, c_s, c_r,
    wx_s, wx_r, wz_s, wz_r, wf_s, wf_r, q_s, q_r, f_s, f_r,
):
    expert = lax.axis_index("expert")
    z = lax.axis_index("dp")
    core = expert % 2
    x = (expert // 2) % RING
    y = expert // (2 * RING)

    def device(dy=0, dx=0, dz=0, dc=0):
        ey, ex, ec = (y + dy) % RING, (x + dx) % RING, (core + dc) % 2
        return ((ey * RING + ex) * 2 + ec, (z + dz) % RING)

    def remote(src, dst, send, recv, to):
        return pltpu.make_async_remote_copy(
            src_ref=src, dst_ref=dst, send_sem=send, recv_sem=recv, device_id=to, device_id_type=MESH
        )

    def pair_copies():
        return (
            remote(routes_ref, listed.at[core], pair_s.at[0], pair_r.at[0], device(dc=1)),
            remote(tok_ref, both.at[pl.ds(core * TOK, TOK)], pair_s.at[1], pair_r.at[1], device(dc=1)),
        )

    def own_copy():
        return pltpu.make_async_copy(tok_ref, both.at[pl.ds(core * TOK, TOK)], own_s)

    def z_copy(k, d):
        first = pl.multiple_of(((z + d) % RING) * BLOCK + k * CHUNK, 128)
        return remote(
            tok_ref.at[:, pl.ds(first, CHUNK)], cols.at[k, core, x, z], z_s.at[k, d - 1], z_r.at[k, d - 1], device(dz=d)
        )

    def z_local(k):
        first = pl.multiple_of(z * BLOCK + k * CHUNK, 128)
        return pltpu.make_async_copy(tok_ref.at[:, pl.ds(first, CHUNK)], cols.at[k, core, x, z], zl_s.at[k])

    def xo_copy(k, way):
        here = cols.at[k, core, x, z]
        return remote(here, here, xo_s.at[k, way], xo_r.at[k, way], device(dx=1 if way == 0 else 3))

    def xa_copy(k, way, d):
        here = cols.at[k, core, x, (z + RING - d) % RING]
        return remote(here, here, xa_s.at[k, way, d - 1], xa_r.at[k, way, d - 1], device(dx=1 if way == 0 else 3))

    def xb_copy(k, way):
        origin = (x + (3 if way == 0 else 1)) % RING
        here = cols.at[k, core, origin, pl.ds(2 * way, 2)]
        return remote(here, here, xb_s.at[k, way], xb_r.at[k, way], device(dx=1 if way == 0 else 3))

    def ca_copy(k, d):
        here = cols.at[k, core, (x + d) % RING]
        return remote(here, here, ca_s.at[k, d % RING], ca_r.at[k, d % RING], device(dc=1))

    def c_copy(k):
        here = cols.at[k, core, (x + 2) % RING]
        return remote(here, here, c_s.at[k], c_r.at[k], device(dc=1))

    def wx_copy(g, d):
        return remote(
            packed.at[g * RING + d], win.at[g, z, x], wx_s.at[g, d - 1], wx_r.at[g, d - 1], device(dx=d)
        )

    def wz_copy(g, way):
        here = win.at[g, z]
        return remote(here, here, wz_s.at[g, way], wz_r.at[g, way], device(dz=1 if way == 0 else 3))

    def wf_copy(g, way):
        origin = (z + (3 if way == 0 else 1)) % RING
        here = win.at[g, origin, pl.ds(2 * way, 2)]
        return remote(here, here, wf_s.at[g, way], wf_r.at[g, way], device(dz=1 if way == 0 else 3))

    def sum_copies(way, slot, k):
        to = device(dy=1 if way == 0 else 3)
        values = remote(quant.at[way, slot, k], got_q.at[way, slot, k], q_s.at[way, slot, k], q_r.at[way, slot, k], to)
        if slot == 1:
            return (values,)
        at = slot // 2
        return (values, remote(scale.at[way, at, k], got_s.at[way, at, k], f_s.at[way, at, k], f_r.at[way, at, k], to))

    barrier = pltpu.get_barrier_semaphore()
    peers = [device(dc=1), device(dy=1), device(dy=3)]
    peers += [device(dx=d) for d in (1, 2, 3)] + [device(dz=d) for d in (1, 2, 3)]
    for peer in peers:
        pl.semaphore_signal(barrier, inc=1, device_id=peer, device_id_type=MESH)
    pl.semaphore_wait(barrier, len(peers))

    def send_z(k):
        for d in (1, 3, 2):
            z_copy(k, d).start()

    for copy in pair_copies():
        copy.start()
    own_copy().start()
    for k in range(3):
        send_z(jnp.int32(k))
    for k in range(CHUNKS):
        z_local(k).start()
    listed[core] = routes_ref[...]

    def take_xo(k):
        z_local(k).wait()
        for way in (0, 1):
            xo_copy(k, way).start()

    def take_xa(k):
        for d in (1, 3, 2):
            z_copy(k, d).wait_recv()
            for way in (0, 1):
                xa_copy(k, way, d).start()

    def take_xb(k):
        for way in (0, 1):
            xo_copy(k, way).wait_recv()
            for d in (1, 2, 3):
                xa_copy(k, way, d).wait_recv()
            xb_copy(k, way).start()
        for d in (0, 1, 3):
            ca_copy(k, d).start()

    def take_c(k):
        for way in (0, 1):
            xb_copy(k, way).wait_recv()
        c_copy(k).start()

    def find_slots(_):
        for copy in pair_copies():
            copy.wait_recv()
        own_copy().wait()
        named = jnp.concatenate([listed[0], listed[1]], axis=1)
        row = lax.broadcasted_iota(jnp.int32, (GROUPS * RING, 2 * TOK), 0)
        group, step = row // RING, row % RING
        away = jnp.where(group == 0, OFFSETS[0], jnp.where(group == 1, OFFSETS[1], jnp.where(group == 2, OFFSETS[2], OFFSETS[3])))
        label = (((y + away) % RING) * RING + (x + step) % RING) * 2 + core
        hit = jnp.zeros((GROUPS * RING, 2 * TOK), jnp.float32)
        for choice in range(named.shape[0]):
            hit += jnp.where(named[choice:choice + 1, :] == label, 1.0, 0.0)
        before = lax.broadcasted_iota(jnp.int32, (2 * TOK, 2 * TOK), 0) < lax.broadcasted_iota(
            jnp.int32, (2 * TOK, 2 * TOK), 1
        )
        rank = jnp.dot(
            hit.astype(jnp.bfloat16), jnp.where(before, 1.0, 0.0).astype(jnp.bfloat16), preferred_element_type=jnp.float32
        )
        slots[...] = jnp.where(hit > 0.0, rank, -1.0)

    def take_p(g):
        slot = lax.broadcasted_iota(jnp.int32, (PAIR, 2 * TOK), 0).astype(jnp.float32)
        source = lax.broadcasted_iota(jnp.int32, (SPAN, 512), 0)
        target = lax.broadcasted_iota(jnp.int32, (SPAN, 512), 1)
        for d in (2, 1, 3, 0):
            row = g * RING + d
            taken = jnp.where(slots[pl.ds(row, 1), :] == slot, 1.0, 0.0).astype(jnp.bfloat16)
            label = (((y + offset_of(g)) % RING) * RING + (x + d) % RING) * 2 + core
            start = start_ref[label]
            tile = jnp.minimum(lax.div(start, jnp.int32(128)), (WIDTH - SPAN) // 128)
            shift = start - tile * 128
            first = tile * 128
            rows = both[:, pl.ds(first, SPAN)]
            picked = jnp.dot(taken, rows, preferred_element_type=jnp.float32)
            moved = jnp.where(source == target + shift, 1.0, 0.0).astype(jnp.bfloat16)
            picked = jnp.dot(picked.astype(jnp.bfloat16), moved, preferred_element_type=jnp.float32)
            rest = picked[:, 384:SLAB]
            seat = slots[pl.ds(row, 1), :]
            seats = [seat[:, 64 * part:64 * part + 64] for part in range(4)] + [jnp.zeros((12, 64), jnp.float32)]
            tail = jnp.concatenate([rest[:TAIL], jnp.concatenate([rest[TAIL:]] + seats, axis=0)], axis=1)
            blocks = [picked[:, 128 * tile:128 * tile + 128] for tile in range(3)] + [tail]
            value = jnp.concatenate(blocks, axis=0).astype(jnp.bfloat16)
            if d == 0:
                win[g, z, x] = value
            else:
                packed[row] = value
                wx_copy(g, d).start()

    def take_wz(g):
        for d in (1, 2, 3):
            wx_copy(g, d).wait_recv()
        for way in (0, 1):
            wz_copy(g, way).start()

    def take_wzf(g):
        for way in (0, 1):
            wz_copy(g, way).wait_recv()
            wf_copy(g, way).start()

    def take_exp(g):
        for way in (0, 1):
            wf_copy(g, way).wait_recv()
        slot = lax.broadcasted_iota(jnp.int32, (PAIR, 2 * TOK), 0).astype(jnp.float32)
        total = jnp.zeros((1, 2 * TOK), jnp.float32)
        rests = []
        for place in range(PLACES):
            tail = win[g, place // RING, place % RING, FULL:, :].astype(jnp.float32)
            first, second = tail[:, :64], tail[:, 64:]
            rests.append(jnp.concatenate([first, second[:PAIR - TAIL]], axis=0))
            at = PAIR - TAIL
            seat = jnp.concatenate([second[at + part:at + part + 1] for part in range(4)], axis=1)
            chosen[g, place] = jnp.where(seat == slot, 1.0, 0.0).astype(jnp.bfloat16)
            total += jnp.where(seat >= 0.0, 1.0, 0.0)
        hits[g] = total
        for tile in range(3):
            block = win[g, :, :, tile * PAIR:(tile + 1) * PAIR, :].reshape(PLACES * PAIR, 128)
            wide[g, tile * 128:(tile + 1) * 128, :] = block.T
        wide[g, 384:, :] = jnp.concatenate(rests, axis=0).astype(jnp.bfloat16).T

    def scale_row(slot, piece):
        return (slot + 1) // 2, pl.ds(piece + (2 if slot == 1 else 0), 1)

    def restored(way, slot, k, piece):
        block = got_q[way, slot, k, pl.ds(piece * SCALE_ROWS, SCALE_ROWS), :]
        at, row = scale_row(slot, piece)
        return block.astype(jnp.int32).astype(jnp.float32) * got_s[way, at, k, row, :]

    def send_sum(way, slot, k, pieces, count):
        for piece, block in enumerate(pieces):
            most = jnp.max(jnp.abs(block), axis=0, keepdims=True)
            factor = jnp.where(most > 0.0, 32767.0 / jnp.where(most > 0.0, most, 1.0), 0.0)
            rows = pl.ds(piece * SCALE_ROWS, SCALE_ROWS)
            quant[way, slot, k, rows, :] = jnp.round(block * factor).astype(jnp.int32).astype(jnp.int16)
            at, row = scale_row(slot, piece)
            scale[way, at, k, row, :] = most * (1.0 / 32767.0)
        if count is not None:
            scale[way, slot // 2, k, pl.ds(7, 1), :] = count
        for copy in sum_copies(way, slot, k):
            copy.start()

    def take_u(unit):
        g, k = unit // CHUNKS, unit % CHUNKS

        @pl.when(g == 0)
        def _():
            for d in (0, 1, 3):
                ca_copy(k, d).wait_recv()
            c_copy(k).wait_recv()

        for place in range(PLACES):
            from_x, from_z = place % RING, place // RING
            tokens = jnp.concatenate([cols[k, 0, from_x, from_z], cols[k, 1, from_x, from_z]], axis=0)
            near[pl.ds(place * PAIR, PAIR), :] = jnp.dot(
                chosen[g, place], tokens, preferred_element_type=jnp.float32
            ).astype(jnp.bfloat16)
        part[...] = jnp.dot(wide[g], near[...], preferred_element_type=jnp.float32)

        def pieces(half):
            first = half * HALF
            return [part[first + SCALE_ROWS * piece:first + SCALE_ROWS * (piece + 1), :] for piece in range(2)]

        @pl.when(g == 0)
        def _():
            for way in (0, 1):
                send_sum(way, 0, k, pieces(way), hits[g])

        for way in (0, 1):
            @pl.when(g == 1 + way)
            def _():
                send_sum(way, 1, k, pieces(1 - way), None)
                kept[way, k] = part[way * HALF:(way + 1) * HALF, :]

        @pl.when(g == 3)
        def _():
            out_ref[:, pl.ds(pl.multiple_of(k * CHUNK, 128), CHUNK)] = part[...]

    def take_v(unit):
        k = unit % CHUNKS
        for way in (0, 1):
            @pl.when(unit // CHUNKS == way)
            def _():
                for copy in sum_copies(way, 0, k):
                    copy.wait_recv()
                pieces = [
                    kept[way, k, pl.ds(piece * SCALE_ROWS, SCALE_ROWS), :] + restored(way, 0, k, piece)
                    for piece in range(2)
                ]
                below = got_s[way, 0, k, pl.ds(7, 1), :]
                send_sum(way, 2, k, pieces, hits[1] + below if way == 0 else hits[2])

    actions = {
        "S": find_slots, "P": take_p, "XO": take_xo, "XA": take_xa, "XB": take_xb, "Z": send_z, "WZ": take_wz,
        "WZF": take_wzf, "C": take_c, "EXP": take_exp, "U": take_u, "V": take_v,
    }
    words, length = plan()

    def one_step(step, carry):
        code = looked_up(words, step)

        def among(names):
            if len(names) == 1:
                actions[names[0]](code - CODES[names[0]])
                return
            middle = len(names) // 2
            low = code < CODES[names[middle]]
            pl.when(low)(lambda: among(names[:middle]))
            pl.when(jnp.logical_not(low))(lambda: among(names[middle:]))

        among(list(CODES))
        return carry

    lax.fori_loop(0, length, one_step, 0)

    def finish(k, carry):
        for way in (0, 1):
            for slot in (1, 2):
                for copy in sum_copies(way, slot, k):
                    copy.wait_recv()
        count = hits[3] + got_s[0, 1, k, pl.ds(7, 1), :] + got_s[1, 1, k, pl.ds(7, 1), :]
        inverse = 1.0 / jnp.sum(count, axis=1, keepdims=True)
        at = pl.ds(pl.multiple_of(k * CHUNK, 128), CHUNK)
        for half in (0, 1):
            for piece in (0, 1):
                rows = pl.ds(half * HALF + piece * SCALE_ROWS, SCALE_ROWS)
                total = out_ref[rows, at] + restored(half, 2, k, piece) + restored(1 - half, 1, k, piece)
                out_ref[rows, at] = total * inverse
        return carry

    lax.fori_loop(0, CHUNKS, finish, 0)

    for copy in pair_copies():
        copy.wait_send()

    def drain(k, carry):
        for d in (1, 2, 3):
            z_copy(k, d).wait_send()
            for way in (0, 1):
                xa_copy(k, way, d).wait_send()
        for d in (0, 1, 3):
            ca_copy(k, d).wait_send()
        c_copy(k).wait_send()
        for way in (0, 1):
            xo_copy(k, way).wait_send()
            xb_copy(k, way).wait_send()
            for slot in range(3):
                for copy in sum_copies(way, slot, k):
                    copy.wait_send()
        return carry

    lax.fori_loop(0, CHUNKS, drain, 0)

    def drain_windows(g, carry):
        for d in (1, 2, 3):
            wx_copy(g, d).wait_send()
        for way in (0, 1):
            wz_copy(g, way).wait_send()
            wf_copy(g, way).wait_send()
        return carry

    lax.fori_loop(0, GROUPS, drain_windows, 0)


def shards(tokens, routes, slab_start):
    dma = pltpu.SemaphoreType.DMA
    bf16, f32, i16 = jnp.bfloat16, jnp.float32, jnp.int16
    result = pl.pallas_call(
        gram_kernel,
        out_shape=pltpu.VMEM((SLAB, BLOCK), f32),
        in_specs=[
            pl.BlockSpec(memory_space=pltpu.SMEM),
            pl.BlockSpec(memory_space=pltpu.VMEM),
            pl.BlockSpec(memory_space=pl.ANY),
        ],
        out_specs=pl.BlockSpec(memory_space=pltpu.VMEM),
        scratch_shapes=[
            pltpu.VMEM((2 * TOK, WIDTH), bf16),
            pltpu.VMEM((2, 8, TOK), jnp.int32),
            pltpu.VMEM((GROUPS * RING, 2 * TOK), f32),
            pltpu.VMEM((GROUPS * RING, FULL + TAIL, 128), bf16),
            pltpu.VMEM((GROUPS, RING, RING, FULL + TAIL, 128), bf16),
            pltpu.VMEM((GROUPS, PLACES, PAIR, 2 * TOK), bf16),
            pltpu.VMEM((GROUPS, SLAB, PLACES * PAIR), bf16),
            pltpu.VMEM((CHUNKS, 2, RING, RING, TOK, CHUNK), bf16),
            pltpu.VMEM((PLACES * PAIR, CHUNK), bf16),
            pltpu.VMEM((SLAB, CHUNK), f32),
            pltpu.VMEM((2, CHUNKS, HALF, CHUNK), f32),
            pltpu.VMEM((2, 3, CHUNKS, HALF, CHUNK), i16),
            pltpu.VMEM((2, 2, CHUNKS, 8, CHUNK), f32),
            pltpu.VMEM((2, 3, CHUNKS, HALF, CHUNK), i16),
            pltpu.VMEM((2, 2, CHUNKS, 8, CHUNK), f32),
            pltpu.VMEM((GROUPS, 1, 2 * TOK), f32),
            dma((2,)), dma((2,)), dma(()),
            dma((CHUNKS, 3)), dma((CHUNKS, 3)), dma((CHUNKS,)),
            dma((CHUNKS, 2)), dma((CHUNKS, 2)), dma((CHUNKS, 2, 3)), dma((CHUNKS, 2, 3)), dma((CHUNKS, 2)), dma((CHUNKS, 2)),
            dma((CHUNKS, 4)), dma((CHUNKS, 4)), dma((CHUNKS,)), dma((CHUNKS,)),
            dma((GROUPS, 3)), dma((GROUPS, 3)), dma((GROUPS, 2)), dma((GROUPS, 2)), dma((GROUPS, 2)), dma((GROUPS, 2)),
            dma((2, 3, CHUNKS)), dma((2, 3, CHUNKS)), dma((2, 2, CHUNKS)), dma((2, 2, CHUNKS)),
        ],
        compiler_params=pltpu.CompilerParams(
            collective_id=0, has_side_effects=True, vmem_limit_bytes=56 * 2**20
        ),
        name="gram",
    )(slab_start, routes.T, tokens)
    return result[None]


def solution(mesh):
    placed = (P(("expert", "dp"), None), P(("expert", "dp"), None), P())
    return jax.shard_map(
        shards, mesh=mesh, in_specs=placed, out_specs=P("expert", None, "dp"), check_vma=False
    )
```

time: 118 us -> 114 us (0.966); the launches traced: 117 us -> 114 us
  Pallas kernels: 115 us -> 113 us
    pallas_call x1, Pallas kernels: 115 us -> 113 us  [shards(): pl.pallas_call(gram_kernel, out_shape=pltpu.VMEM((SLAB, BLOCK), f32), in_...]
where the time goes in v3:
time: 114 us
  Pallas kernels  113 us (99%)
  local copies, waits for them, and re-layouts  1.69 us (1%)
    pallas_call x1, Pallas kernels, shards(): pl.pallas_call(gram_kernel, out_shape=pltpu.VMEM((SLAB, BLOCK), f32), in_...  113 us

profile of v3, /device:TPU:1, one launch (start us, length us, event | category | flops | bytes accessed | tf_op | source)
XLA Modules:
  0.0 114.2 jit_solution(4945762142022732991)
XLA Ops:
  0.0 112.5 %gram.1 = f32[448,1792]{1,0:T(8,128)S(1)} custom-call(s32[32]{0:T(128)} %start_ref.1, s32[8,128]{1,0:T(8,128)} %bitcast.3, bf16[128,7168]{1,0:T(8,128)(2,1)} %tok_ref.1), custom_call_target="tpu_custom_call" | custom-call | tf_op jit(solution)/shard_map/gram/pallas_call | solution.py:419
  112.5 1.7 %copy.5 = f32[1,448,1792]{2,1,0:T(8,128)} copy(f32[1,448,1792]{2,1,0:T(8,128)S(1)} %bitcast.2) | data formatting | bytes 6422528

commit v4 on v3

--- a/solution.py
+++ b/solution.py
@@ -28,12 +28,12 @@
     "U": 0, "V": 28, "XO": 42, "XA": 49, "XB": 56, "C": 63, "Z": 70, "P": 77, "WZ": 81, "WZF": 85, "EXP": 89, "S": 93,
 }
 SCHEDULE = (
-    "XO1", "XO5", "Z5", "XO4", "XO0", "S0", "P0", "P2", "WZ0", "P1", "WZ2", "XA1", "WZF0", "XA5", "XA0", "WZ1",
-    "WZF2", "XB5", "XB1", "XB0", "P3", "C5", "EXP0", "XO2", "C1", "XA2", "U05", "WZF1", "XO6", "C0", "U01", "Z4",
-    "EXP2", "U25", "U00", "Z6", "EXP1", "U15", "U10", "XB2", "V05", "V15", "U20", "XA4", "U21", "C2", "XA6", "WZ3",
-    "V11", "U11", "U02", "V10", "V01", "XB4", "Z3", "XB6", "XO3", "V00", "U12", "U22", "C4", "V02", "XA3", "WZF3",
-    "C6", "V12", "U06", "U04", "U26", "XB3", "U16", "U24", "U14", "V16", "C3", "EXP3", "U32", "U03", "U23", "U34",
-    "V04", "U13", "U30", "V06", "V03", "V13", "U36", "U31", "V14", "U35", "U33",
+    "XO1", "XO2", "XO0", "Z5", "XA0", "S0", "P0", "P2", "XB0", "WZ0", "XA1", "WZ2", "WZF0", "C0", "P1", "XA2",
+    "XB1", "WZ1", "WZF2", "EXP0", "U00", "XB2", "XO5", "P3", "C1", "WZF1", "Z4", "XO4", "XO3", "XA5", "C2", "U01",
+    "EXP2", "U02", "U21", "EXP1", "U11", "XA4", "V11", "V01", "Z3", "U10", "V00", "U20", "XB5", "Z6", "U22", "XB4",
+    "U12", "XO6", "V10", "C5", "V12", "WZ3", "V02", "XA3", "XA6", "C4", "U05", "U25", "U04", "U15", "WZF3", "U14",
+    "XB3", "U24", "V05", "V04", "XB6", "V15", "EXP3", "V14", "C3", "U34", "U35", "C6", "U03", "U13", "U06", "U23",
+    "U33", "V03", "V13", "U32", "U16", "U26", "V16", "V06", "U30", "U36", "U31",
 )
 
 
@@ -129,14 +129,13 @@
             packed.at[g * RING + d], win.at[g, z, x], wx_s.at[g, d - 1], wx_r.at[g, d - 1], device(dx=d)
         )
 
-    def wz_copy(g, way):
-        here = win.at[g, z]
-        return remote(here, here, wz_s.at[g, way], wz_r.at[g, way], device(dz=1 if way == 0 else 3))
-
-    def wf_copy(g, way):
-        origin = (z + (3 if way == 0 else 1)) % RING
-        here = win.at[g, origin, pl.ds(2 * way, 2)]
-        return remote(here, here, wf_s.at[g, way], wf_r.at[g, way], device(dz=1 if way == 0 else 3))
+    def wz_copy(g, way, d):
+        here = win.at[g, z, (x + RING - d) % RING]
+        return remote(here, here, wz_s.at[g, way, d], wz_r.at[g, way, d], device(dz=1 if way == 0 else 3))
+
+    def wf_copy(g, way, d):
+        here = win.at[g, (z + (3 if way == 0 else 1)) % RING, (x + RING - d) % RING]
+        return remote(here, here, wf_s.at[g, way, d % 2], wf_r.at[g, way, d % 2], device(dz=1 if way == 0 else 3))
 
     def sum_copies(way, slot, k):
         to = device(dy=1 if way == 0 else 3)
@@ -146,6 +145,10 @@
         at = slot // 2
         return (values, remote(scale.at[way, at, k], got_s.at[way, at, k], f_s.at[way, at, k], f_r.at[way, at, k], to))
 
+    for k in range(CHUNKS):
+        z_local(k).start()
+    own_copy().start()
+
     barrier = pltpu.get_barrier_semaphore()
     peers = [device(dc=1), device(dy=1), device(dy=3)]
     peers += [device(dx=d) for d in (1, 2, 3)] + [device(dz=d) for d in (1, 2, 3)]
@@ -159,11 +162,8 @@
 
     for copy in pair_copies():
         copy.start()
-    own_copy().start()
     for k in range(3):
         send_z(jnp.int32(k))
-    for k in range(CHUNKS):
-        z_local(k).start()
     listed[core] = routes_ref[...]
 
     def take_xo(k):
@@ -235,24 +235,29 @@
             value = jnp.concatenate(blocks, axis=0).astype(jnp.bfloat16)
             if d == 0:
                 win[g, z, x] = value
+                for way in (0, 1):
+                    wz_copy(g, way, 0).start()
             else:
                 packed[row] = value
                 wx_copy(g, d).start()
 
     def take_wz(g):
-        for d in (1, 2, 3):
+        for d in (1, 3, 2):
             wx_copy(g, d).wait_recv()
-        for way in (0, 1):
-            wz_copy(g, way).start()
+            for way in (0, 1):
+                wz_copy(g, way, d).start()
 
     def take_wzf(g):
         for way in (0, 1):
-            wz_copy(g, way).wait_recv()
-            wf_copy(g, way).start()
+            for d in (2 * way, 2 * way + 1):
+                wz_copy(g, way, d).wait_recv()
+                wf_copy(g, way, d).start()
 
     def take_exp(g):
         for way in (0, 1):
-            wf_copy(g, way).wait_recv()
+            for d in (2 * way, 2 * way + 1):
+                wz_copy(g, 1 - way, d).wait_recv()
+                wf_copy(g, way, d).wait_recv()
         slot = lax.broadcasted_iota(jnp.int32, (PAIR, 2 * TOK), 0).astype(jnp.float32)
         total = jnp.zeros((1, 2 * TOK), jnp.float32)
         rests = []
@@ -264,7 +269,7 @@
             seat = jnp.concatenate([second[at + part:at + part + 1] for part in range(4)], axis=1)
             chosen[g, place] = jnp.where(seat == slot, 1.0, 0.0).astype(jnp.bfloat16)
             total += jnp.where(seat >= 0.0, 1.0, 0.0)
-        hits[g] = total
+        hits[g] = total[:, :TOK] + total[:, TOK:]
         for tile in range(3):
             block = win[g, :, :, tile * PAIR:(tile + 1) * PAIR, :].reshape(PLACES * PAIR, 128)
             wide[g, tile * 128:(tile + 1) * 128, :] = block.T
@@ -276,12 +281,15 @@
     def restored(way, slot, k, piece):
         block = got_q[way, slot, k, pl.ds(piece * SCALE_ROWS, SCALE_ROWS), :]
         at, row = scale_row(slot, piece)
-        return block.astype(jnp.int32).astype(jnp.float32) * got_s[way, at, k, row, :]
+        factor = got_s[way, at, k, row, :]
+        return block.astype(jnp.int32).astype(jnp.float32) * jnp.concatenate([factor, factor], axis=1)
 
     def send_sum(way, slot, k, pieces, count):
         for piece, block in enumerate(pieces):
             most = jnp.max(jnp.abs(block), axis=0, keepdims=True)
+            most = jnp.maximum(most[:, :128], most[:, 128:])
             factor = jnp.where(most > 0.0, 32767.0 / jnp.where(most > 0.0, most, 1.0), 0.0)
+            factor = jnp.concatenate([factor, factor], axis=1)
             rows = pl.ds(piece * SCALE_ROWS, SCALE_ROWS)
             quant[way, slot, k, rows, :] = jnp.round(block * factor).astype(jnp.int32).astype(jnp.int16)
             at, row = scale_row(slot, piece)
@@ -406,8 +414,10 @@
         for d in (1, 2, 3):
             wx_copy(g, d).wait_send()
         for way in (0, 1):
-            wz_copy(g, way).wait_send()
-            wf_copy(g, way).wait_send()
+            for d in range(RING):
+                wz_copy(g, way, d).wait_send()
+            for d in (2 * way, 2 * way + 1):
+                wf_copy(g, way, d).wait_send()
         return carry
 
     lax.fori_loop(0, GROUPS, drain_windows, 0)
@@ -438,15 +448,15 @@
             pltpu.VMEM((SLAB, CHUNK), f32),
             pltpu.VMEM((2, CHUNKS, HALF, CHUNK), f32),
             pltpu.VMEM((2, 3, CHUNKS, HALF, CHUNK), i16),
-            pltpu.VMEM((2, 2, CHUNKS, 8, CHUNK), f32),
+            pltpu.VMEM((2, 2, CHUNKS, 8, 128), f32),
             pltpu.VMEM((2, 3, CHUNKS, HALF, CHUNK), i16),
-            pltpu.VMEM((2, 2, CHUNKS, 8, CHUNK), f32),
-            pltpu.VMEM((GROUPS, 1, 2 * TOK), f32),
+            pltpu.VMEM((2, 2, CHUNKS, 8, 128), f32),
+            pltpu.VMEM((GROUPS, 1, TOK), f32),
             dma((2,)), dma((2,)), dma(()),
             dma((CHUNKS, 3)), dma((CHUNKS, 3)), dma((CHUNKS,)),
             dma((CHUNKS, 2)), dma((CHUNKS, 2)), dma((CHUNKS, 2, 3)), dma((CHUNKS, 2, 3)), dma((CHUNKS, 2)), dma((CHUNKS, 2)),
             dma((CHUNKS, 4)), dma((CHUNKS, 4)), dma((CHUNKS,)), dma((CHUNKS,)),
-            dma((GROUPS, 3)), dma((GROUPS, 3)), dma((GROUPS, 2)), dma((GROUPS, 2)), dma((GROUPS, 2)), dma((GROUPS, 2)),
+            dma((GROUPS, 3)), dma((GROUPS, 3)), dma((GROUPS, 2, RING)), dma((GROUPS, 2, RING)), dma((GROUPS, 2, 2)), dma((GROUPS, 2, 2)),
             dma((2, 3, CHUNKS)), dma((2, 3, CHUNKS)), dma((2, 2, CHUNKS)), dma((2, 2, CHUNKS)),
         ],
         compiler_params=pltpu.CompilerParams(

time: 114 us -> 107 us (0.939)
  Pallas kernels: 113 us -> 106 us
    pallas_call x1, Pallas kernels: 113 us -> 106 us  [shards(): pl.pallas_call(gram_kernel, out_shape=pltpu.VMEM((SLAB, BLOCK), f32), in_...]
where the time goes in v4:
time: 107 us
  Pallas kernels  106 us (99%)
  local copies, waits for them, and re-layouts  1.69 us (2%)
    pallas_call x1, Pallas kernels, shards(): pl.pallas_call(gram_kernel, out_shape=pltpu.VMEM((SLAB, BLOCK), f32), in_...  106 us

profile of v4, /device:TPU:1, one launch (start us, length us, event | category | flops | bytes accessed | tf_op | source)
XLA Modules:
  0.0 107.3 jit_solution(7599460080108372571)
XLA Ops:
  0.0 105.6 %gram.1 = f32[448,1792]{1,0:T(8,128)S(1)} custom-call(s32[32]{0:T(128)} %start_ref.1, s32[8,128]{1,0:T(8,128)} %bitcast.3, bf16[128,7168]{1,0:T(8,128)(2,1)} %tok_ref.1), custom_call_target="tpu_custom_call" | custom-call | tf_op jit(solution)/shard_map/gram/pallas_call | solution.py:429
  105.6 1.7 %copy.5 = f32[1,448,1792]{2,1,0:T(8,128)} copy(f32[1,448,1792]{2,1,0:T(8,128)S(1)} %bitcast.2) | data formatting | bytes 6422528

commit v5 on v4

--- a/solution.py
+++ b/solution.py
@@ -47,6 +47,14 @@
     padded = codes + [0] * (-len(codes) % 4)
     words = [sum(padded[at + i] * 128 ** i for i in range(4)) for at in range(0, len(padded), 4)]
     return words, len(codes)
+
+
+def finish_word():
+    last = {}
+    for at, item in enumerate(SCHEDULE):
+        if item[0] == "V" or item[:2] in ("U1", "U2"):
+            last[int(item[2])] = at
+    return sum(k * 16 ** place for place, k in enumerate(sorted(last, key=last.get)))
 
 
 def looked_up(words, step):
@@ -259,21 +267,25 @@
                 wz_copy(g, 1 - way, d).wait_recv()
                 wf_copy(g, way, d).wait_recv()
         slot = lax.broadcasted_iota(jnp.int32, (PAIR, 2 * TOK), 0).astype(jnp.float32)
+        low = lax.broadcasted_iota(jnp.int32, (1, 128), 1) < 64
         total = jnp.zeros((1, 2 * TOK), jnp.float32)
-        rests = []
+        seats = win[g, :, :, FULL + PAIR - TAIL:, :].reshape(PLACES * 16, 128).astype(jnp.float32)[:, 64:]
+        seats = jnp.concatenate([seats, seats], axis=1)
         for place in range(PLACES):
-            tail = win[g, place // RING, place % RING, FULL:, :].astype(jnp.float32)
-            first, second = tail[:, :64], tail[:, 64:]
-            rests.append(jnp.concatenate([first, second[:PAIR - TAIL]], axis=0))
-            at = PAIR - TAIL
-            seat = jnp.concatenate([second[at + part:at + part + 1] for part in range(4)], axis=1)
+            rows = [seats[16 * place + part:16 * place + part + 1] for part in range(4)]
+            seat = jnp.concatenate([jnp.where(low, rows[0], rows[1]), jnp.where(low, rows[2], rows[3])], axis=1)
             chosen[g, place] = jnp.where(seat == slot, 1.0, 0.0).astype(jnp.bfloat16)
             total += jnp.where(seat >= 0.0, 1.0, 0.0)
         hits[g] = total[:, :TOK] + total[:, TOK:]
+        split = PLACES * TAIL
         for tile in range(3):
-            block = win[g, :, :, tile * PAIR:(tile + 1) * PAIR, :].reshape(PLACES * PAIR, 128)
-            wide[g, tile * 128:(tile + 1) * 128, :] = block.T
-        wide[g, 384:, :] = jnp.concatenate(rests, axis=0).astype(jnp.bfloat16).T
+            at = tile * PAIR
+            block = win[g, :, :, at:at + TAIL, :].reshape(split, 128)
+            wide[g, tile * 128:(tile + 1) * 128, :split] = block.T
+            block = win[g, :, :, at + TAIL:at + PAIR, :].reshape(PLACES * (PAIR - TAIL), 128)
+            wide[g, tile * 128:(tile + 1) * 128, split:] = block.T
+        wide[g, 384:, :split] = win[g, :, :, FULL:, :].reshape(split, 128).T[:64]
+        wide[g, 384:, split:] = win[g, :, :, FULL:FULL + PAIR - TAIL, :].reshape(PLACES * (PAIR - TAIL), 128).T[64:]
 
     def scale_row(slot, piece):
         return (slot + 1) // 2, pl.ds(piece + (2 if slot == 1 else 0), 1)
@@ -311,9 +323,9 @@
         for place in range(PLACES):
             from_x, from_z = place % RING, place // RING
             tokens = jnp.concatenate([cols[k, 0, from_x, from_z], cols[k, 1, from_x, from_z]], axis=0)
-            near[pl.ds(place * PAIR, PAIR), :] = jnp.dot(
-                chosen[g, place], tokens, preferred_element_type=jnp.float32
-            ).astype(jnp.bfloat16)
+            picked = jnp.dot(chosen[g, place], tokens, preferred_element_type=jnp.float32).astype(jnp.bfloat16)
+            near[pl.ds(place * TAIL, TAIL), :] = picked[:TAIL]
+            near[pl.ds(PLACES * TAIL + place * (PAIR - TAIL), PAIR - TAIL), :] = picked[TAIL:]
         part[...] = jnp.dot(wide[g], near[...], preferred_element_type=jnp.float32)
 
         def pieces(half):
@@ -372,7 +384,40 @@
 
     lax.fori_loop(0, length, one_step, 0)
 
-    def finish(k, carry):
+    def drain(k, carry):
+        for d in (1, 2, 3):
+            z_copy(k, d).wait_send()
+            for way in (0, 1):
+                xa_copy(k, way, d).wait_send()
+        for d in (0, 1, 3):
+            ca_copy(k, d).wait_send()
+        c_copy(k).wait_send()
+        for way in (0, 1):
+            xo_copy(k, way).wait_send()
+            xb_copy(k, way).wait_send()
+        return carry
+
+    def drain_windows(g, carry):
+        for d in (1, 2, 3):
+            wx_copy(g, d).wait_send()
+        for way in (0, 1):
+            for d in range(RING):
+                wz_copy(g, way, d).wait_send()
+            for d in (2 * way, 2 * way + 1):
+                wf_copy(g, way, d).wait_send()
+        return carry
+
+    for copy in pair_copies():
+        copy.wait_send()
+    lax.fori_loop(0, CHUNKS, drain, 0)
+    lax.fori_loop(0, GROUPS, drain_windows, 0)
+
+    def finish(place, carry):
+        k = lax.shift_right_logical(jnp.int32(finish_word()), 4 * place) % 16
+        for way in (0, 1):
+            for slot in range(3):
+                for copy in sum_copies(way, slot, k):
+                    copy.wait_send()
         for way in (0, 1):
             for slot in (1, 2):
                 for copy in sum_copies(way, slot, k):
@@ -388,39 +433,6 @@
         return carry
 
     lax.fori_loop(0, CHUNKS, finish, 0)
-
-    for copy in pair_copies():
-        copy.wait_send()
-
-    def drain(k, carry):
-        for d in (1, 2, 3):
-            z_copy(k, d).wait_send()
-            for way in (0, 1):
-                xa_copy(k, way, d).wait_send()
-        for d in (0, 1, 3):
-            ca_copy(k, d).wait_send()
-        c_copy(k).wait_send()
-        for way in (0, 1):
-            xo_copy(k, way).wait_send()
-            xb_copy(k, way).wait_send()
-            for slot in range(3):
-                for copy in sum_copies(way, slot, k):
-                    copy.wait_send()
-        return carry
-
-    lax.fori_loop(0, CHUNKS, drain, 0)
-
-    def drain_windows(g, carry):
-        for d in (1, 2, 3):
-            wx_copy(g, d).wait_send()
-        for way in (0, 1):
-            for d in range(RING):
-                wz_copy(g, way, d).wait_send()
-            for d in (2 * way, 2 * way + 1):
-                wf_copy(g, way, d).wait_send()
-        return carry
-
-    lax.fori_loop(0, GROUPS, drain_windows, 0)
 
 
 def shards(tokens, routes, slab_start):

time: 107 us -> 107 us (level)
  no operation moved by 1% of the time
where the time goes in v5:
time: 107 us
  Pallas kernels  105 us (98%)
  local copies, waits for them, and re-layouts  1.69 us (2%)
    pallas_call x1, Pallas kernels, shards(): pl.pallas_call(gram_kernel, out_shape=pltpu.VMEM((SLAB, BLOCK), f32), in_...  105 us

profile of v5, /device:TPU:1, one launch (start us, length us, event | category | flops | bytes accessed | tf_op | source)
XLA Modules:
  0.0 106.9 jit_solution(1765633701741404287)
XLA Ops:
  0.0 105.2 %gram.1 = f32[448,1792]{1,0:T(8,128)S(1)} custom-call(s32[32]{0:T(128)} %start_ref.1, s32[8,128]{1,0:T(8,128)} %bitcast.3, bf16[128,7168]{1,0:T(8,128)(2,1)} %tok_ref.1), custom_call_target="tpu_custom_call" | custom-call | tf_op jit(solution)/shard_map/gram/pallas_call | solution.py:441
  105.3 1.7 %copy.5 = f32[1,448,1792]{2,1,0:T(8,128)} copy(f32[1,448,1792]{2,1,0:T(8,128)S(1)} %bitcast.2) | data formatting | bytes 6422528

commit v6 on v5

--- a/solution.py
+++ b/solution.py
@@ -28,12 +28,12 @@
     "U": 0, "V": 28, "XO": 42, "XA": 49, "XB": 56, "C": 63, "Z": 70, "P": 77, "WZ": 81, "WZF": 85, "EXP": 89, "S": 93,
 }
 SCHEDULE = (
-    "XO1", "XO2", "XO0", "Z5", "XA0", "S0", "P0", "P2", "XB0", "WZ0", "XA1", "WZ2", "WZF0", "C0", "P1", "XA2",
-    "XB1", "WZ1", "WZF2", "EXP0", "U00", "XB2", "XO5", "P3", "C1", "WZF1", "Z4", "XO4", "XO3", "XA5", "C2", "U01",
-    "EXP2", "U02", "U21", "EXP1", "U11", "XA4", "V11", "V01", "Z3", "U10", "V00", "U20", "XB5", "Z6", "U22", "XB4",
-    "U12", "XO6", "V10", "C5", "V12", "WZ3", "V02", "XA3", "XA6", "C4", "U05", "U25", "U04", "U15", "WZF3", "U14",
-    "XB3", "U24", "V05", "V04", "XB6", "V15", "EXP3", "V14", "C3", "U34", "U35", "C6", "U03", "U13", "U06", "U23",
-    "U33", "V03", "V13", "U32", "U16", "U26", "V16", "V06", "U30", "U36", "U31",
+    "XO1", "XO0", "XO4", "Z4", "XA0", "S0", "P0", "P1", "XA1", "P2", "WZ0", "XB0", "XA4", "WZ1", "WZF0", "C0",
+    "WZ2", "WZF1", "XB1", "EXP0", "XB4", "XO2", "XA2", "XO6", "U00", "C1", "WZF2", "P3", "C4", "U01", "EXP1", "U10",
+    "U04", "EXP2", "Z5", "U21", "XB2", "V00", "XO5", "U20", "Z6", "V11", "U14", "XA5", "U24", "V04", "C2", "U11",
+    "XA6", "V01", "Z3", "WZ3", "V10", "U02", "XB5", "V14", "U22", "U12", "XB6", "XO3", "V12", "C5", "XA3", "WZF3",
+    "V02", "U05", "C6", "U15", "U25", "EXP3", "U06", "XB3", "V15", "U36", "V05", "U16", "U26", "C3", "V06", "U32",
+    "V16", "U30", "U03", "U23", "U13", "U35", "U33", "U34", "V03", "V13", "U31",
 )
 
 
@@ -221,8 +221,8 @@
 
     def take_p(g):
         slot = lax.broadcasted_iota(jnp.int32, (PAIR, 2 * TOK), 0).astype(jnp.float32)
-        source = lax.broadcasted_iota(jnp.int32, (SPAN, 512), 0)
-        target = lax.broadcasted_iota(jnp.int32, (SPAN, 512), 1)
+        source = lax.broadcasted_iota(jnp.int32, (SPAN, SLAB), 0)
+        target = lax.broadcasted_iota(jnp.int32, (SPAN, SLAB), 1)
         for d in (2, 1, 3, 0):
             row = g * RING + d
             taken = jnp.where(slots[pl.ds(row, 1), :] == slot, 1.0, 0.0).astype(jnp.bfloat16)

time: 107 us -> 107 us (level)
  no operation moved by 1% of the time
where the time goes in v6:
time: 107 us
  Pallas kernels  105 us (98%)
  local copies, waits for them, and re-layouts  1.69 us (2%)
    pallas_call x1, Pallas kernels, shards(): pl.pallas_call(gram_kernel, out_shape=pltpu.VMEM((SLAB, BLOCK), f32), in_...  105 us

profile of v6, /device:TPU:1, one launch (start us, length us, event | category | flops | bytes accessed | tf_op | source)
XLA Modules:
  0.0 106.6 jit_solution(15809646901848842212)
XLA Ops:
  0.0 104.9 %gram.1 = f32[448,1792]{1,0:T(8,128)S(1)} custom-call(s32[32]{0:T(128)} %start_ref.1, s32[8,128]{1,0:T(8,128)} %bitcast.3, bf16[128,7168]{1,0:T(8,128)(2,1)} %tok_ref.1), custom_call_target="tpu_custom_call" | custom-call | tf_op jit(solution)/shard_map/gram/pallas_call | solution.py:441
  104.9 1.7 %copy.5 = f32[1,448,1792]{2,1,0:T(8,128)} copy(f32[1,448,1792]{2,1,0:T(8,128)S(1)} %bitcast.2) | data formatting | bytes 6422528

commit v7 on v6

--- a/solution.py
+++ b/solution.py
@@ -168,9 +168,10 @@
         for d in (1, 3, 2):
             z_copy(k, d).start()
 
+    send_z(jnp.int32(0))
     for copy in pair_copies():
         copy.start()
-    for k in range(3):
+    for k in (1, 2):
         send_z(jnp.int32(k))
     listed[core] = routes_ref[...]
 

time: 107 us -> 107 us (level)
  no operation moved by 1% of the time
where the time goes in v7:
time: 107 us
  Pallas kernels  105 us (98%)
  local copies, waits for them, and re-layouts  1.69 us (2%)
    pallas_call x1, Pallas kernels, shards(): pl.pallas_call(gram_kernel, out_shape=pltpu.VMEM((SLAB, BLOCK), f32), in_...  105 us

profile of v7, /device:TPU:1, one launch (start us, length us, event | category | flops | bytes accessed | tf_op | source)
XLA Modules:
  0.0 106.6 jit_solution(5985098191587233299)
XLA Ops:
  0.0 104.9 %gram.1 = f32[448,1792]{1,0:T(8,128)S(1)} custom-call(s32[32]{0:T(128)} %start_ref.1, s32[8,128]{1,0:T(8,128)} %bitcast.3, bf16[128,7168]{1,0:T(8,128)(2,1)} %tok_ref.1), custom_call_target="tpu_custom_call" | custom-call | tf_op jit(solution)/shard_map/gram/pallas_call | solution.py:442
  104.9 1.7 %copy.5 = f32[1,448,1792]{2,1,0:T(8,128)} copy(f32[1,448,1792]{2,1,0:T(8,128)S(1)} %bitcast.2) | data formatting | bytes 6422528
